TPU v7x, 32 devices: a whole 2x2x4 slice. The times are simulated.
32 devices in a mesh: sec: 4 (over y, x), gx: 4 (over z), gz: 2 (over core).
Axes of the slice: x: 2, y: 2, z: 4, core: 2. Of those that a mesh axis runs over, the one named last changes fastest.
Arguments:
- fields: float32 [4, 5, 512, 256], P('sec', None, 'gx', 'gz'), may hold values from -6 to 6
- media: float32 [4, 3, 512, 256], P('sec', None, 'gx', 'gz'), may hold values from 0.5 to 2
- plane_rows: int32 [16], replicated, may hold values from 0 to 255, as said below
- box_offset: int32 [3], replicated, may hold values from 0 to 128
Outputs:
- evolved: float32 [4, 5, 512, 256], P('sec', None, 'gx', 'gz')
Inputs may be any that keep to these rules, and one draw needn't show every extreme that they name: `plane_rows`: entries 8 * j to 8 * j + 7 are distinct rows of the j-th depth block of 128 rows; row 0 and row 255 are always among them.
All inputs are finite; a program needn't handle non-finite values.
Results may differ from a plain program's by a relative error of at most 0.00013.
Values sent between devices are 32-bit elements; how exact they have to be, the bound alone decides.
No kernel may reach another device: no remote copies, remote signals or barrier semaphores. Data moves between devices by JAX's collectives and lax.ppermute only.
A program may use at most 64 MiB of HBM per device.

v0:
```python
import jax
import jax.numpy as jnp
from jax import lax
from jax.sharding import PartitionSpec as P

RADIUS = 4
STEPS = 5
NPD = 8


STENCIL = (0.8, -0.2, 4.0 / 105.0, -1.0 / 280.0)
TIME_STEP = 0.2
COUPLING = 0.5
RELAXATION = (0.9, 0.5)
MEMORY_WEIGHT = (0.15, 0.1)


def padded_2(block, sides, width):
    for axis, dim in sides:
        count = lax.axis_size(axis)
        forward = [(i, i + 1) for i in range(count - 1)]
        backward = [(target, source) for source, target in forward]
        low = lax.ppermute(
            lax.slice_in_dim(block, block.shape[dim] - width, None, axis=dim), axis, forward
        )
        high = lax.ppermute(lax.slice_in_dim(block, 0, width, axis=dim), axis, backward)
        block = jnp.concatenate([low, block, high], axis=dim)
    return block


def broadcast(value, axis, source):
    kept = jnp.where(lax.axis_index(axis) == source, value, 0).astype(value.dtype)
    return lax.psum(kept, axis)


def along_x(padded, anchor, count_x, count_z):
    summed = jnp.zeros(padded.shape[:-2] + (count_x, count_z), jnp.float32)
    for offset, stencil_tap in enumerate(STENCIL, 1):
        forward = padded[
            ..., anchor + offset : anchor + offset + count_x, anchor : anchor + count_z
        ]
        backward = padded[
            ..., anchor - offset : anchor - offset + count_x, anchor : anchor + count_z
        ]
        summed = summed + stencil_tap * (forward - backward)
    return summed


def along_z(padded, anchor, count_x, count_z):
    summed = jnp.zeros(padded.shape[:-2] + (count_x, count_z), jnp.float32)
    for offset, stencil_tap in enumerate(STENCIL, 1):
        forward = padded[
            ..., anchor : anchor + count_x, anchor + offset : anchor + offset + count_z
        ]
        backward = padded[
            ..., anchor : anchor + count_x, anchor - offset : anchor - offset + count_z
        ]
        summed = summed + stencil_tap * (forward - backward)
    return summed


def velocity_elastic(velocity, stresses, buoyancy, anchor, count_x, count_z):
    updated_x = velocity[0] + TIME_STEP * buoyancy * (
        along_x(stresses[0], anchor, count_x, count_z)
        + along_z(stresses[2], anchor, count_x, count_z)
    )
    updated_z = velocity[1] + TIME_STEP * buoyancy * (
        along_x(stresses[2], anchor, count_x, count_z)
        + along_z(stresses[1], anchor, count_x, count_z)
    )
    return jnp.stack([updated_x, updated_z])


def velocity_acoustic(velocity, stresses, buoyancy, anchor, count_x, count_z):
    updated_x = velocity[0] - TIME_STEP * buoyancy * along_x(stresses[0], anchor, count_x, count_z)
    updated_z = velocity[1] - TIME_STEP * buoyancy * along_z(stresses[0], anchor, count_x, count_z)
    return jnp.stack([updated_x, updated_z])


def stress_elastic(stresses, velocity_pad, material, anchor, count_x, count_z):
    strain_x = along_x(velocity_pad[0], anchor, count_x, count_z)
    strain_z = along_z(velocity_pad[1], anchor, count_x, count_z)
    strain_shear = along_z(velocity_pad[0], anchor, count_x, count_z) + along_x(
        velocity_pad[1], anchor, count_x, count_z
    )
    lame_first = material[1]
    shear_modulus = material[2]
    normal_x = stresses[0] + TIME_STEP * (
        (lame_first + 2.0 * shear_modulus) * strain_x + lame_first * strain_z
    )
    normal_z = stresses[1] + TIME_STEP * (
        lame_first * strain_x + (lame_first + 2.0 * shear_modulus) * strain_z
    )
    shear_new = stresses[2] + TIME_STEP * shear_modulus * strain_shear
    return jnp.stack([normal_x, normal_z, shear_new])


def stress_acoustic(stresses, velocity_pad, material, anchor, count_x, count_z):
    divergence = along_x(velocity_pad[0], anchor, count_x, count_z) + along_z(
        velocity_pad[1], anchor, count_x, count_z
    )
    loading = material[1] * divergence
    memory_one = (
        RELAXATION[0] * stresses[1]
        + (1.0 - RELAXATION[0]) * MEMORY_WEIGHT[0] * material[2] * loading
    )
    memory_two = (
        RELAXATION[1] * stresses[2]
        + (1.0 - RELAXATION[1]) * MEMORY_WEIGHT[1] * material[2] * loading
    )
    pressure = stresses[0] - TIME_STEP * (loading - memory_one - memory_two)
    return jnp.stack([pressure, memory_one, memory_two])


def local(fields, media, plane_rows, box_offset):
    current = fields[0]
    material = media[0]
    count_x = current.shape[1]
    count_z = current.shape[2]
    section = lax.axis_index("sec")
    is_source = section == 0
    block_z = lax.axis_index("gz")
    local_rows = lax.dynamic_slice_in_dim(plane_rows, block_z * NPD, NPD) - block_z * count_z
    offset = lax.dynamic_slice_in_dim(box_offset, jnp.maximum(section - 1, 0), 1)[0]
    depth_ids = block_z * count_z + jnp.arange(count_z, dtype=jnp.int32)
    landing = offset + plane_rows // 2
    chosen = (landing[:, None] == depth_ids[None, :]).astype(jnp.float32)
    for step_index in range(STEPS):
        stress_pad = padded_2(current[2:5], (("gx", 1), ("gz", 2)), RADIUS)
        velocity = lax.cond(
            is_source,
            lambda: velocity_elastic(
                current[0:2], stress_pad, material[0], RADIUS, count_x, count_z
            ),
            lambda: velocity_acoustic(
                current[0:2], stress_pad, material[0], RADIUS, count_x, count_z
            ),
        )
        velocity_pad = padded_2(velocity, (("gx", 1), ("gz", 2)), RADIUS)
        stresses = lax.cond(
            is_source,
            lambda: stress_elastic(current[2:5], velocity_pad, material, RADIUS, count_x, count_z),
            lambda: stress_acoustic(current[2:5], velocity_pad, material, RADIUS, count_x, count_z),
        )
        current = jnp.concatenate([velocity, stresses], axis=0)
        picked = jnp.take(current, local_rows, axis=2)
        block_plane = jnp.transpose(
            jnp.stack([picked[0], picked[1], -0.5 * (picked[2] + picked[3])]), (0, 2, 1)
        )
        joined = lax.all_gather(block_plane, "gz", axis=1, tiled=True)
        gathered = broadcast(joined, "sec", 0)
        injected = jnp.einsum("ckx,kz->cxz", gathered, chosen, precision=lax.Precision.HIGHEST)
        far_state = jnp.concatenate([current[0:3] + COUPLING * injected, current[3:5]], axis=0)
        current = jnp.where(is_source, current, far_state)
    return current[None]


def solution(mesh):
    in_specs = (P("sec", None, "gx", "gz"), P("sec", None, "gx", "gz"), P(), P())
    out_specs = P("sec", None, "gx", "gz")
    return jax.shard_map(local, mesh=mesh, in_specs=in_specs, out_specs=out_specs, check_vma=False)
```

profile of v0, /device:TPU:0, one launch (start us, length us, event | category | flops | bytes accessed | tf_op | source)
XLA Modules:
  0.0 230.6 jit_solution(7828171862898087966)
XLA Ops:
  1.0 4.9 %collective-permute-start = (f32[3,4,128]{2,1,0:T(4,128)S(1)}, f32[3,4,128]{2,1,0:T(4,128)S(1)}, u32[]{:S(2)}, u32[]{:S(2)}) collective-permute-start(f32[3,4,128]{2,1,0:T(4,128)S(1)} %get-tuple-element.306), channel_id=1, source_target_pairs={{0,2},{2,4},{4,6},{1,3},{3,5},{5,7},{8,10},{10,12},{12,14},{9,11},... | collective-permute-start | bytes 18440 | tf_op jit(solution)/shard_map/ppermute | solution.py:23
  14.3 2.0 collective-permute-done.3
  17.2 3.5 %collective-permute-start.4 = (f32[2,4,128]{2,1,0:T(4,128)S(1)}, f32[2,4,128]{2,1,0:T(4,128)S(1)}, u32[]{:S(2)}, u32[]{:S(2)}) collective-permute-start(f32[2,4,128]{2,1,0:T(4,128)S(1)} %get-tuple-element.326), channel_id=1, source_target_pairs={{0,2},{2,4},{4,6},{1,3},{3,5},{5,7},{8,10},{10,12},{12,14},{9,11},... | collective-permute-start | bytes 12296 | tf_op jit(solution)/shard_map/ppermute | solution.py:23
  22.1 4.2 %collective-permute-done.5 = f32[2,4,128]{2,1,0:T(4,128)S(1)} collective-permute-done((f32[2,4,128]{2,1,0:T(4,128)S(1)}, f32[2,4,128]{2,1,0:T(4,128)S(1)}, u32[]{:S(2)}, u32[]{:S(2)}) %collective-permute-start.5) | collective-permute-done | bytes 4128 | tf_op jit(solution)/shard_map/ppermute | solution.py:26
  29.0 1.9 collective-permute-done.7
  34.6 15.7 %psum.35 = f32[3,16,128]{2,1,0:T(8,128)S(1)} all-reduce(f32[3,16,128]{2,1,0:T(8,128)S(1)} %broadcast_select_fusion.4), channel_id=1, replica_groups=mesh['sec'=4,'gx'=4,'gz'=2] {'sec'}, use_global_device_ids=true, to_apply=%region_4.6 | all-reduce | flops 6144 | bytes 49152 | tf_op jit(solution)/shard_map/psum | solution.py:33
  50.7 3.5 %collective-permute-start.8 = (f32[3,4,128]{2,1,0:T(4,128)S(1)}, f32[3,4,128]{2,1,0:T(4,128)S(1)}, u32[]{:S(2)}, u32[]{:S(2)}) collective-permute-start(f32[3,4,128]{2,1,0:T(4,128)S(1)} %get-tuple-element.294), channel_id=1, source_target_pairs={{0,2},{2,4},{4,6},{1,3},{3,5},{5,7},{8,10},{10,12},{12,14},{9,11},... | collective-permute-start | bytes 18440 | tf_op jit(solution)/shard_map/ppermute | solution.py:23
  55.6 4.2 %collective-permute-done.9 = f32[3,4,128]{2,1,0:T(4,128)S(1)} collective-permute-done((f32[3,4,128]{2,1,0:T(4,128)S(1)}, f32[3,4,128]{2,1,0:T(4,128)S(1)}, u32[]{:S(2)}, u32[]{:S(2)}) %collective-permute-start.9) | collective-permute-done | bytes 6176 | tf_op jit(solution)/shard_map/ppermute | solution.py:26
  62.5 2.0 collective-permute-done.11
  65.6 2.9 %collective-permute-start.12 = (f32[2,4,128]{2,1,0:T(4,128)S(1)}, f32[2,4,128]{2,1,0:T(4,128)S(1)}, u32[]{:S(2)}, u32[]{:S(2)}) collective-permute-start(f32[2,4,128]{2,1,0:T(4,128)S(1)} %get-tuple-element.324), channel_id=1, source_target_pairs={{0,2},{2,4},{4,6},{1,3},{3,5},{5,7},{8,10},{10,12},{12,14},{9,11},... | collective-permute-start | bytes 12296 | tf_op jit(solution)/shard_map/ppermute | solution.py:23
  69.8 4.2 %collective-permute-done.13 = f32[2,4,128]{2,1,0:T(4,128)S(1)} collective-permute-done((f32[2,4,128]{2,1,0:T(4,128)S(1)}, f32[2,4,128]{2,1,0:T(4,128)S(1)}, u32[]{:S(2)}, u32[]{:S(2)}) %collective-permute-start.13) | collective-permute-done | bytes 4128 | tf_op jit(solution)/shard_map/ppermute | solution.py:26
  76.7 1.9 collective-permute-done.15
  82.4 14.0 %psum.36 = f32[3,16,128]{2,1,0:T(8,128)S(1)} all-reduce(f32[3,16,128]{2,1,0:T(8,128)S(1)} %broadcast_select_fusion.3), channel_id=1, replica_groups=mesh['sec'=4,'gx'=4,'gz'=2] {'sec'}, use_global_device_ids=true, to_apply=%region_9.11 | all-reduce | flops 6144 | bytes 49152 | tf_op jit(solution)/shard_map/psum | solution.py:33
  96.8 1.9 collective-permute-start.16
  100.1 4.2 %collective-permute-done.17 = f32[3,4,128]{2,1,0:T(4,128)S(1)} collective-permute-done((f32[3,4,128]{2,1,0:T(4,128)S(1)}, f32[3,4,128]{2,1,0:T(4,128)S(1)}, u32[]{:S(2)}, u32[]{:S(2)}) %collective-permute-start.17) | collective-permute-done | bytes 6176 | tf_op jit(solution)/shard_map/ppermute | solution.py:26
  107.1 2.0 collective-permute-done.19
  110.1 1.9 collective-permute-start.20
  113.3 4.2 %collective-permute-done.21 = f32[2,4,128]{2,1,0:T(4,128)S(1)} collective-permute-done((f32[2,4,128]{2,1,0:T(4,128)S(1)}, f32[2,4,128]{2,1,0:T(4,128)S(1)}, u32[]{:S(2)}, u32[]{:S(2)}) %collective-permute-start.21) | collective-permute-done | bytes 4128 | tf_op jit(solution)/shard_map/ppermute | solution.py:26
  120.3 1.9 collective-permute-done.23
  126.1 15.1 %psum.37 = f32[3,16,128]{2,1,0:T(8,128)S(1)} all-reduce(f32[3,16,128]{2,1,0:T(8,128)S(1)} %broadcast_select_fusion.2), channel_id=1, replica_groups=mesh['sec'=4,'gx'=4,'gz'=2] {'sec'}, use_global_device_ids=true, to_apply=%region_14.16 | all-reduce | flops 6144 | bytes 49152 | tf_op jit(solution)/shard_map/psum | solution.py:33
  141.7 1.9 collective-permute-start.24
  144.9 4.2 %collective-permute-done.25 = f32[3,4,128]{2,1,0:T(4,128)S(1)} collective-permute-done((f32[3,4,128]{2,1,0:T(4,128)S(1)}, f32[3,4,128]{2,1,0:T(4,128)S(1)}, u32[]{:S(2)}, u32[]{:S(2)}) %collective-permute-start.25) | collective-permute-done | bytes 6176 | tf_op jit(solution)/shard_map/ppermute | solution.py:26
  151.9 2.0 collective-permute-done.27
  154.9 1.9 collective-permute-start.28
  158.2 4.2 %collective-permute-done.29 = f32[2,4,128]{2,1,0:T(4,128)S(1)} collective-permute-done((f32[2,4,128]{2,1,0:T(4,128)S(1)}, f32[2,4,128]{2,1,0:T(4,128)S(1)}, u32[]{:S(2)}, u32[]{:S(2)}) %collective-permute-start.29) | collective-permute-done | bytes 4128 | tf_op jit(solution)/shard_map/ppermute | solution.py:26
  165.1 1.9 collective-permute-done.31
  170.8 14.0 %psum.38 = f32[3,16,128]{2,1,0:T(8,128)S(1)} all-reduce(f32[3,16,128]{2,1,0:T(8,128)S(1)} %broadcast_select_fusion.1), channel_id=1, replica_groups=mesh['sec'=4,'gx'=4,'gz'=2] {'sec'}, use_global_device_ids=true, to_apply=%region_19.21 | all-reduce | flops 6144 | bytes 49152 | tf_op jit(solution)/shard_map/psum | solution.py:33
  188.4 4.2 %collective-permute-done.33 = f32[3,4,128]{2,1,0:T(4,128)S(1)} collective-permute-done((f32[3,4,128]{2,1,0:T(4,128)S(1)}, f32[3,4,128]{2,1,0:T(4,128)S(1)}, u32[]{:S(2)}, u32[]{:S(2)}) %collective-permute-start.33) | collective-permute-done | bytes 6176 | tf_op jit(solution)/shard_map/ppermute | solution.py:26
  195.4 2.0 collective-permute-done.35
  201.6 4.2 %collective-permute-done.37 = f32[2,4,128]{2,1,0:T(4,128)S(1)} collective-permute-done((f32[2,4,128]{2,1,0:T(4,128)S(1)}, f32[2,4,128]{2,1,0:T(4,128)S(1)}, u32[]{:S(2)}, u32[]{:S(2)}) %collective-permute-start.37) | collective-permute-done | bytes 4128 | tf_op jit(solution)/shard_map/ppermute | solution.py:26
  208.6 1.9 collective-permute-done.39
  214.2 15.2 %psum.39 = f32[3,16,128]{2,1,0:T(8,128)S(1)} all-reduce(f32[3,16,128]{2,1,0:T(8,128)S(1)} %broadcast_select_fusion), channel_id=1, replica_groups=mesh['sec'=4,'gx'=4,'gz'=2] {'sec'}, use_global_device_ids=true, to_apply=%region_24.26 | all-reduce | flops 6144 | bytes 49152 | tf_op jit(solution)/shard_map/psum | solution.py:33
  (226 shorter events, 82.6 us)
Async XLA Ops:
  1.0 8.8 %collective-permute-start = (f32[3,4,128]{2,1,0:T(4,128)S(1)}, f32[3,4,128]{2,1,0:T(4,128)S(1)}, u32[]{:S(2)}, u32[]{:S(2)}) collective-permute-start(f32[3,4,128]{2,1,0:T(4,128)S(1)} %get-tuple-element.306), channel_id=1, source_target_pairs={{0,2},{2,4},{4,6},{1,3},{3,5},{5,7},{8,10},{10,12},{12,14},{9,11},... | collective-permute-start | bytes 18440 | tf_op jit(solution)/shard_map/ppermute | solution.py:23
  5.9 5.5 %collective-permute-start.1 = (f32[3,4,128]{2,1,0:T(4,128)S(1)}, f32[3,4,128]{2,1,0:T(4,128)S(1)}, u32[]{:S(2)}, u32[]{:S(2)}) collective-permute-start(f32[3,4,128]{2,1,0:T(4,128)S(1)} %get-tuple-element.307), channel_id=1, source_target_pairs={{2,0},{4,2},{6,4},{3,1},{5,3},{7,5},{10,8},{12,10},{14,12},{11,9},... | collective-permute-start | bytes 18440 | tf_op jit(solution)/shard_map/ppermute | solution.py:26
  11.6 2.7 %collective-permute-start.2 = (f32[3,136,4]{2,1,0:T(8,128)S(1)}, f32[3,136,4]{2,1,0:T(8,128)S(1)}, u32[]{:S(2)}, u32[]{:S(2)}) collective-permute-start(f32[3,136,4]{2,1,0:T(8,128)S(1)} %get-tuple-element.304), channel_id=1, source_target_pairs={{0,1},{2,3},{4,5},{6,7},{8,9},{10,11},{12,13},{14,15},{16,17},{18,... | collective-permute-start | bytes 19592 | tf_op jit(solution)/shard_map/ppermute | solution.py:23
  12.9 3.4 %collective-permute-start.3 = (f32[3,136,4]{2,1,0:T(8,128)S(1)}, f32[3,136,4]{2,1,0:T(8,128)S(1)}, u32[]{:S(2)}, u32[]{:S(2)}) collective-permute-start(f32[3,136,4]{2,1,0:T(8,128)S(1)} %get-tuple-element.305), channel_id=1, source_target_pairs={{1,0},{3,2},{5,4},{7,6},{9,8},{11,10},{13,12},{15,14},{17,16},{19,... | collective-permute-start | bytes 19592 | tf_op jit(solution)/shard_map/ppermute | solution.py:26
  17.2 4.8 %collective-permute-start.4 = (f32[2,4,128]{2,1,0:T(4,128)S(1)}, f32[2,4,128]{2,1,0:T(4,128)S(1)}, u32[]{:S(2)}, u32[]{:S(2)}) collective-permute-start(f32[2,4,128]{2,1,0:T(4,128)S(1)} %get-tuple-element.326), channel_id=1, source_target_pairs={{0,2},{2,4},{4,6},{1,3},{3,5},{5,7},{8,10},{10,12},{12,14},{9,11},... | collective-permute-start | bytes 12296 | tf_op jit(solution)/shard_map/ppermute | solution.py:23
  20.7 5.5 %collective-permute-start.5 = (f32[2,4,128]{2,1,0:T(4,128)S(1)}, f32[2,4,128]{2,1,0:T(4,128)S(1)}, u32[]{:S(2)}, u32[]{:S(2)}) collective-permute-start(f32[2,4,128]{2,1,0:T(4,128)S(1)} %get-tuple-element.327), channel_id=1, source_target_pairs={{2,0},{4,2},{6,4},{3,1},{5,3},{7,5},{10,8},{12,10},{14,12},{11,9},... | collective-permute-start | bytes 12296 | tf_op jit(solution)/shard_map/ppermute | solution.py:26
  26.4 2.6 %collective-permute-start.6 = (f32[2,136,4]{2,1,0:T(8,128)S(1)}, f32[2,136,4]{2,1,0:T(8,128)S(1)}, u32[]{:S(2)}, u32[]{:S(2)}) collective-permute-start(f32[2,136,4]{2,1,0:T(8,128)S(1)} %get-tuple-element.316), channel_id=1, source_target_pairs={{0,1},{2,3},{4,5},{6,7},{8,9},{10,11},{12,13},{14,15},{16,17},{18,... | collective-permute-start | bytes 13064 | tf_op jit(solution)/shard_map/ppermute | solution.py:23
  27.7 3.3 %collective-permute-start.7 = (f32[2,136,4]{2,1,0:T(8,128)S(1)}, f32[2,136,4]{2,1,0:T(8,128)S(1)}, u32[]{:S(2)}, u32[]{:S(2)}) collective-permute-start(f32[2,136,4]{2,1,0:T(8,128)S(1)} %get-tuple-element.317), channel_id=1, source_target_pairs={{1,0},{3,2},{5,4},{7,6},{9,8},{11,10},{13,12},{15,14},{17,16},{19,... | collective-permute-start | bytes 13064 | tf_op jit(solution)/shard_map/ppermute | solution.py:26
  50.7 4.8 %collective-permute-start.8 = (f32[3,4,128]{2,1,0:T(4,128)S(1)}, f32[3,4,128]{2,1,0:T(4,128)S(1)}, u32[]{:S(2)}, u32[]{:S(2)}) collective-permute-start(f32[3,4,128]{2,1,0:T(4,128)S(1)} %get-tuple-element.294), channel_id=1, source_target_pairs={{0,2},{2,4},{4,6},{1,3},{3,5},{5,7},{8,10},{10,12},{12,14},{9,11},... | collective-permute-start | bytes 18440 | tf_op jit(solution)/shard_map/ppermute | solution.py:23
  54.2 5.5 %collective-permute-start.9 = (f32[3,4,128]{2,1,0:T(4,128)S(1)}, f32[3,4,128]{2,1,0:T(4,128)S(1)}, u32[]{:S(2)}, u32[]{:S(2)}) collective-permute-start(f32[3,4,128]{2,1,0:T(4,128)S(1)} %get-tuple-element.295), channel_id=1, source_target_pairs={{2,0},{4,2},{6,4},{3,1},{5,3},{7,5},{10,8},{12,10},{14,12},{11,9},... | collective-permute-start | bytes 18440 | tf_op jit(solution)/shard_map/ppermute | solution.py:26
  61.2 3.4 %collective-permute-start.11 = (f32[3,136,4]{2,1,0:T(8,128)S(1)}, f32[3,136,4]{2,1,0:T(8,128)S(1)}, u32[]{:S(2)}, u32[]{:S(2)}) collective-permute-start(f32[3,136,4]{2,1,0:T(8,128)S(1)} %get-tuple-element.303), channel_id=1, source_target_pairs={{1,0},{3,2},{5,4},{7,6},{9,8},{11,10},{13,12},{15,14},{17,16},{19,... | collective-permute-start | bytes 19592 | tf_op jit(solution)/shard_map/ppermute | solution.py:26
  65.6 4.2 %collective-permute-start.12 = (f32[2,4,128]{2,1,0:T(4,128)S(1)}, f32[2,4,128]{2,1,0:T(4,128)S(1)}, u32[]{:S(2)}, u32[]{:S(2)}) collective-permute-start(f32[2,4,128]{2,1,0:T(4,128)S(1)} %get-tuple-element.324), channel_id=1, source_target_pairs={{0,2},{2,4},{4,6},{1,3},{3,5},{5,7},{8,10},{10,12},{12,14},{9,11},... | collective-permute-start | bytes 12296 | tf_op jit(solution)/shard_map/ppermute | solution.py:23
  68.5 5.5 %collective-permute-start.13 = (f32[2,4,128]{2,1,0:T(4,128)S(1)}, f32[2,4,128]{2,1,0:T(4,128)S(1)}, u32[]{:S(2)}, u32[]{:S(2)}) collective-permute-start(f32[2,4,128]{2,1,0:T(4,128)S(1)} %get-tuple-element.325), channel_id=1, source_target_pairs={{2,0},{4,2},{6,4},{3,1},{5,3},{7,5},{10,8},{12,10},{14,12},{11,9},... | collective-permute-start | bytes 12296 | tf_op jit(solution)/shard_map/ppermute | solution.py:26
  75.4 3.3 %collective-permute-start.15 = (f32[2,136,4]{2,1,0:T(8,128)S(1)}, f32[2,136,4]{2,1,0:T(8,128)S(1)}, u32[]{:S(2)}, u32[]{:S(2)}) collective-permute-start(f32[2,136,4]{2,1,0:T(8,128)S(1)} %get-tuple-element.315), channel_id=1, source_target_pairs={{1,0},{3,2},{5,4},{7,6},{9,8},{11,10},{13,12},{15,14},{17,16},{19,... | collective-permute-start | bytes 13064 | tf_op jit(solution)/shard_map/ppermute | solution.py:26
  96.8 3.3 %collective-permute-start.16 = (f32[3,4,128]{2,1,0:T(4,128)S(1)}, f32[3,4,128]{2,1,0:T(4,128)S(1)}, u32[]{:S(2)}, u32[]{:S(2)}) collective-permute-start(f32[3,4,128]{2,1,0:T(4,128)S(1)} %get-tuple-element.292), channel_id=1, source_target_pairs={{0,2},{2,4},{4,6},{1,3},{3,5},{5,7},{8,10},{10,12},{12,14},{9,11},... | collective-permute-start | bytes 18440 | tf_op jit(solution)/shard_map/ppermute | solution.py:23
  98.8 5.5 %collective-permute-start.17 = (f32[3,4,128]{2,1,0:T(4,128)S(1)}, f32[3,4,128]{2,1,0:T(4,128)S(1)}, u32[]{:S(2)}, u32[]{:S(2)}) collective-permute-start(f32[3,4,128]{2,1,0:T(4,128)S(1)} %get-tuple-element.293), channel_id=1, source_target_pairs={{2,0},{4,2},{6,4},{3,1},{5,3},{7,5},{10,8},{12,10},{14,12},{11,9},... | collective-permute-start | bytes 18440 | tf_op jit(solution)/shard_map/ppermute | solution.py:26
  105.7 3.4 %collective-permute-start.19 = (f32[3,136,4]{2,1,0:T(8,128)S(1)}, f32[3,136,4]{2,1,0:T(8,128)S(1)}, u32[]{:S(2)}, u32[]{:S(2)}) collective-permute-start(f32[3,136,4]{2,1,0:T(8,128)S(1)} %get-tuple-element.301), channel_id=1, source_target_pairs={{1,0},{3,2},{5,4},{7,6},{9,8},{11,10},{13,12},{15,14},{17,16},{19,... | collective-permute-start | bytes 19592 | tf_op jit(solution)/shard_map/ppermute | solution.py:26
  110.1 3.2 %collective-permute-start.20 = (f32[2,4,128]{2,1,0:T(4,128)S(1)}, f32[2,4,128]{2,1,0:T(4,128)S(1)}, u32[]{:S(2)}, u32[]{:S(2)}) collective-permute-start(f32[2,4,128]{2,1,0:T(4,128)S(1)} %get-tuple-element.322), channel_id=1, source_target_pairs={{0,2},{2,4},{4,6},{1,3},{3,5},{5,7},{8,10},{10,12},{12,14},{9,11},... | collective-permute-start | bytes 12296 | tf_op jit(solution)/shard_map/ppermute | solution.py:23
  112.0 5.5 %collective-permute-start.21 = (f32[2,4,128]{2,1,0:T(4,128)S(1)}, f32[2,4,128]{2,1,0:T(4,128)S(1)}, u32[]{:S(2)}, u32[]{:S(2)}) collective-permute-start(f32[2,4,128]{2,1,0:T(4,128)S(1)} %get-tuple-element.323), channel_id=1, source_target_pairs={{2,0},{4,2},{6,4},{3,1},{5,3},{7,5},{10,8},{12,10},{14,12},{11,9},... | collective-permute-start | bytes 12296 | tf_op jit(solution)/shard_map/ppermute | solution.py:26
  119.0 3.3 %collective-permute-start.23 = (f32[2,136,4]{2,1,0:T(8,128)S(1)}, f32[2,136,4]{2,1,0:T(8,128)S(1)}, u32[]{:S(2)}, u32[]{:S(2)}) collective-permute-start(f32[2,136,4]{2,1,0:T(8,128)S(1)} %get-tuple-element.313), channel_id=1, source_target_pairs={{1,0},{3,2},{5,4},{7,6},{9,8},{11,10},{13,12},{15,14},{17,16},{19,... | collective-permute-start | bytes 13064 | tf_op jit(solution)/shard_map/ppermute | solution.py:26
  141.7 3.3 %collective-permute-start.24 = (f32[3,4,128]{2,1,0:T(4,128)S(1)}, f32[3,4,128]{2,1,0:T(4,128)S(1)}, u32[]{:S(2)}, u32[]{:S(2)}) collective-permute-start(f32[3,4,128]{2,1,0:T(4,128)S(1)} %get-tuple-element.290), channel_id=1, source_target_pairs={{0,2},{2,4},{4,6},{1,3},{3,5},{5,7},{8,10},{10,12},{12,14},{9,11},... | collective-permute-start | bytes 18440 | tf_op jit(solution)/shard_map/ppermute | solution.py:23
  143.6 5.5 %collective-permute-start.25 = (f32[3,4,128]{2,1,0:T(4,128)S(1)}, f32[3,4,128]{2,1,0:T(4,128)S(1)}, u32[]{:S(2)}, u32[]{:S(2)}) collective-permute-start(f32[3,4,128]{2,1,0:T(4,128)S(1)} %get-tuple-element.291), channel_id=1, source_target_pairs={{2,0},{4,2},{6,4},{3,1},{5,3},{7,5},{10,8},{12,10},{14,12},{11,9},... | collective-permute-start | bytes 18440 | tf_op jit(solution)/shard_map/ppermute | solution.py:26
  150.6 3.4 %collective-permute-start.27 = (f32[3,136,4]{2,1,0:T(8,128)S(1)}, f32[3,136,4]{2,1,0:T(8,128)S(1)}, u32[]{:S(2)}, u32[]{:S(2)}) collective-permute-start(f32[3,136,4]{2,1,0:T(8,128)S(1)} %get-tuple-element.299), channel_id=1, source_target_pairs={{1,0},{3,2},{5,4},{7,6},{9,8},{11,10},{13,12},{15,14},{17,16},{19,... | collective-permute-start | bytes 19592 | tf_op jit(solution)/shard_map/ppermute | solution.py:26
  154.9 3.2 %collective-permute-start.28 = (f32[2,4,128]{2,1,0:T(4,128)S(1)}, f32[2,4,128]{2,1,0:T(4,128)S(1)}, u32[]{:S(2)}, u32[]{:S(2)}) collective-permute-start(f32[2,4,128]{2,1,0:T(4,128)S(1)} %get-tuple-element.320), channel_id=1, source_target_pairs={{0,2},{2,4},{4,6},{1,3},{3,5},{5,7},{8,10},{10,12},{12,14},{9,11},... | collective-permute-start | bytes 12296 | tf_op jit(solution)/shard_map/ppermute | solution.py:23
  156.8 5.5 %collective-permute-start.29 = (f32[2,4,128]{2,1,0:T(4,128)S(1)}, f32[2,4,128]{2,1,0:T(4,128)S(1)}, u32[]{:S(2)}, u32[]{:S(2)}) collective-permute-start(f32[2,4,128]{2,1,0:T(4,128)S(1)} %get-tuple-element.321), channel_id=1, source_target_pairs={{2,0},{4,2},{6,4},{3,1},{5,3},{7,5},{10,8},{12,10},{14,12},{11,9},... | collective-permute-start | bytes 12296 | tf_op jit(solution)/shard_map/ppermute | solution.py:26
  163.8 3.3 %collective-permute-start.31 = (f32[2,136,4]{2,1,0:T(8,128)S(1)}, f32[2,136,4]{2,1,0:T(8,128)S(1)}, u32[]{:S(2)}, u32[]{:S(2)}) collective-permute-start(f32[2,136,4]{2,1,0:T(8,128)S(1)} %get-tuple-element.311), channel_id=1, source_target_pairs={{1,0},{3,2},{5,4},{7,6},{9,8},{11,10},{13,12},{15,14},{17,16},{19,... | collective-permute-start | bytes 13064 | tf_op jit(solution)/shard_map/ppermute | solution.py:26
  185.1 3.3 %collective-permute-start.32 = (f32[3,4,128]{2,1,0:T(4,128)S(1)}, f32[3,4,128]{2,1,0:T(4,128)S(1)}, u32[]{:S(2)}, u32[]{:S(2)}) collective-permute-start(f32[3,4,128]{2,1,0:T(4,128)S(1)} %get-tuple-element.288), channel_id=1, source_target_pairs={{0,2},{2,4},{4,6},{1,3},{3,5},{5,7},{8,10},{10,12},{12,14},{9,11},... | collective-permute-start | bytes 18440 | tf_op jit(solution)/shard_map/ppermute | solution.py:23
  187.1 5.5 %collective-permute-start.33 = (f32[3,4,128]{2,1,0:T(4,128)S(1)}, f32[3,4,128]{2,1,0:T(4,128)S(1)}, u32[]{:S(2)}, u32[]{:S(2)}) collective-permute-start(f32[3,4,128]{2,1,0:T(4,128)S(1)} %get-tuple-element.289), channel_id=1, source_target_pairs={{2,0},{4,2},{6,4},{3,1},{5,3},{7,5},{10,8},{12,10},{14,12},{11,9},... | collective-permute-start | bytes 18440 | tf_op jit(solution)/shard_map/ppermute | solution.py:26
  194.1 3.4 %collective-permute-start.35 = (f32[3,136,4]{2,1,0:T(8,128)S(1)}, f32[3,136,4]{2,1,0:T(8,128)S(1)}, u32[]{:S(2)}, u32[]{:S(2)}) collective-permute-start(f32[3,136,4]{2,1,0:T(8,128)S(1)} %get-tuple-element.297), channel_id=1, source_target_pairs={{1,0},{3,2},{5,4},{7,6},{9,8},{11,10},{13,12},{15,14},{17,16},{19,... | collective-permute-start | bytes 19592 | tf_op jit(solution)/shard_map/ppermute | solution.py:26
  198.4 3.2 %collective-permute-start.36 = (f32[2,4,128]{2,1,0:T(4,128)S(1)}, f32[2,4,128]{2,1,0:T(4,128)S(1)}, u32[]{:S(2)}, u32[]{:S(2)}) collective-permute-start(f32[2,4,128]{2,1,0:T(4,128)S(1)} %get-tuple-element.318), channel_id=1, source_target_pairs={{0,2},{2,4},{4,6},{1,3},{3,5},{5,7},{8,10},{10,12},{12,14},{9,11},... | collective-permute-start | bytes 12296 | tf_op jit(solution)/shard_map/ppermute | solution.py:23
  200.3 5.5 %collective-permute-start.37 = (f32[2,4,128]{2,1,0:T(4,128)S(1)}, f32[2,4,128]{2,1,0:T(4,128)S(1)}, u32[]{:S(2)}, u32[]{:S(2)}) collective-permute-start(f32[2,4,128]{2,1,0:T(4,128)S(1)} %get-tuple-element.319), channel_id=1, source_target_pairs={{2,0},{4,2},{6,4},{3,1},{5,3},{7,5},{10,8},{12,10},{14,12},{11,9},... | collective-permute-start | bytes 12296 | tf_op jit(solution)/shard_map/ppermute | solution.py:26
  207.3 3.3 %collective-permute-start.39 = (f32[2,136,4]{2,1,0:T(8,128)S(1)}, f32[2,136,4]{2,1,0:T(8,128)S(1)}, u32[]{:S(2)}, u32[]{:S(2)}) collective-permute-start(f32[2,136,4]{2,1,0:T(8,128)S(1)} %get-tuple-element.309), channel_id=1, source_target_pairs={{1,0},{3,2},{5,4},{7,6},{9,8},{11,10},{13,12},{15,14},{17,16},{19,... | collective-permute-start | bytes 13064 | tf_op jit(solution)/shard_map/ppermute | solution.py:26
  (12 other events, 26.6 us)
where the time goes:
time: 232 us; the launch traced here: 231 us
  blocking collectives  83.1 us (36%)
  starting transfers between devices  65.2 us (28%)
  waiting for transfers between devices  59.3 us (26%)
  other arithmetic  11.4 us (5%)
  local copies, waits for them, and re-layouts  8.22 us (4%)
    psum x5, blocking collectives, broadcast(): return lax.psum(kept, axis)  74 us
    ppermute x20, waiting for transfers between devices, padded_2(): lax.ppermute(lax.slice_in_dim(block, 0, width, axis=dim), axis, backward)  59.2 us
    ppermute x20, starting transfers between devices, padded_2(): lax.ppermute(lax.slice_in_dim(block, block.shape[dim] - width, None, axis...  39.3 us
    ppermute x20, starting transfers between devices, padded_2(): lax.ppermute(lax.slice_in_dim(block, 0, width, axis=dim), axis, backward)  25.8 us
    all_gather x5, blocking collectives, local(): joined = lax.all_gather(block_plane, 'gz', axis=1, tiled=True)  9.1 us
  transfers between devices with their start and end apart: 40, of which 20 were waited for; matrix products, arithmetic and copies ran while one was open for 1% of the time, Pallas kernels for 0%

commit v1 on v0

--- a/solution.py
+++ b/solution.py
@@ -1,12 +1,15 @@
+import functools
+
 import jax
 import jax.numpy as jnp
 from jax import lax
+from jax.experimental import pallas as pl
+from jax.experimental.pallas import tpu as pltpu
 from jax.sharding import PartitionSpec as P
 
 RADIUS = 4
 STEPS = 5
 NPD = 8
-
 
 STENCIL = (0.8, -0.2, 4.0 / 105.0, -1.0 / 280.0)
 TIME_STEP = 0.2
@@ -112,7 +115,7 @@
     return jnp.stack([pressure, memory_one, memory_two])
 
 
-def local(fields, media, plane_rows, box_offset):
+def local_stepwise(fields, media, plane_rows, box_offset):
     current = fields[0]
     material = media[0]
     count_x = current.shape[1]
@@ -155,7 +158,272 @@
     return current[None]
 
 
+HALO = 2 * RADIUS * STEPS
+CELLS = 128
+HALF = CELLS // 2
+WINDOW = HALF + 2 * HALO
+DEPTH = 2 * CELLS
+PART = CELLS - (HALF - HALO)
+NP = 2 * NPD
+TRIM = (0, 0, 16, 16, 32)
+FIRST_ROWS, FIRST_AT = 128, 8
+SECOND_ROWS, SECOND_AT = 96, 24
+ROWS = FIRST_ROWS + SECOND_ROWS
+GROUPS = 8
+SCALE = 840.0
+TAPS = (672.0, -168.0, 32.0, -3.0)
+
+
+def banded(shape, lag):
+    distance = lax.broadcasted_iota(jnp.int32, shape, 0) - lax.broadcasted_iota(
+        jnp.int32, shape, 1
+    )
+    distance = lag * distance
+    values = jnp.zeros(shape, jnp.float32)
+    for offset, tap in enumerate(TAPS, 1):
+        values = jnp.where(distance == offset, tap, values)
+        values = jnp.where(distance == -offset, -tap, values)
+    return values.astype(jnp.bfloat16)
+
+
+def halves(values):
+    high = values.astype(jnp.bfloat16)
+    low = (values - high.astype(jnp.float32)).astype(jnp.bfloat16)
+    return high, low
+
+
+def dot(left, right):
+    return jnp.dot(left, right, preferred_element_type=jnp.float32)
+
+
+def diff_x(band_x, parts):
+    count = parts[0].shape[0]
+    band = band_x[:count, :count]
+    return dot(band, parts[0]) + dot(band, parts[1])
+
+
+def diff_z(band_z, parts):
+    return dot(parts[0], band_z) + dot(parts[1], band_z)
+
+
+def assemble(window, fields, media, ahead, behind, other):
+    core = lax.axis_index("gz")
+
+    @pl.when(core == 0)
+    def _():
+        for index in range(8):
+            own = fields[index] if index < 5 else media[index - 5]
+            window[index, :HALO, :CELLS] = ahead[index]
+            window[index, :HALO, CELLS:] = behind[index]
+            window[index, HALO:, :CELLS] = own[:PART]
+            window[index, HALO:, CELLS:] = other[index]
+
+    @pl.when(core == 1)
+    def _():
+        for index in range(8):
+            own = fields[index] if index < 5 else media[index - 5]
+            window[index, :PART, CELLS:] = own[CELLS - PART :]
+            window[index, :PART, :CELLS] = other[index]
+            window[index, PART:, CELLS:] = ahead[index]
+            window[index, PART:, :CELLS] = behind[index]
+
+
+def trimmed(arrays, amount):
+    if amount == 0:
+        return arrays
+    return [array[amount:-amount] for array in arrays]
+
+
+def place(state, held, sent):
+    start = HALF // 2 + HALF // 4 - HALO
+    core = lax.axis_index("gz")
+    state = [array[start : start + HALF] for array in state]
+
+    @pl.when(core == 0)
+    def _():
+        for index in range(5):
+            held[index, :HALF] = state[index][:, :CELLS]
+            sent[index] = state[index][:, CELLS:]
+
+    @pl.when(core == 1)
+    def _():
+        for index in range(5):
+            held[index, HALF:] = state[index][:, CELLS:]
+            sent[index] = state[index][:, :CELLS]
+
+
+def source_kernel(
+    ids, fields, media, ahead, behind, other, held, sent, rows, window
+):
+    @pl.when(lax.axis_index("sec") == 0)
+    def _():
+        assemble(window, fields, media, ahead, behind, other)
+        band_x = banded((WINDOW, WINDOW), -1)
+        band_z = banded((DEPTH, DEPTH), 1)
+        depth = lax.broadcasted_iota(jnp.int32, (DEPTH, CELLS), 0)
+        pick = jnp.where(depth == ids[0:1, :], 1.0, 0.0).astype(jnp.bfloat16)
+        vx, vz, sxx, szz, sxz, light, lame, shear = [window[index] for index in range(8)]
+        light = light * (TIME_STEP / SCALE)
+        both = (lame + 2.0 * shear) * (TIME_STEP / SCALE)
+        lame = lame * (TIME_STEP / SCALE)
+        shear = shear * (TIME_STEP / SCALE)
+        at = 0
+        for step in range(STEPS):
+            cut = TRIM[step] - at
+            at = TRIM[step]
+            vx, vz, sxx, szz, sxz, light, both, lame, shear = trimmed(
+                [vx, vz, sxx, szz, sxz, light, both, lame, shear], cut
+            )
+            parts_xx, parts_zz, parts_xz = halves(sxx), halves(szz), halves(sxz)
+            vx = vx + light * (diff_x(band_x, parts_xx) + diff_z(band_z, parts_xz))
+            vz = vz + light * (diff_x(band_x, parts_xz) + diff_z(band_z, parts_zz))
+            parts_x, parts_z = halves(vx), halves(vz)
+            strain_x, strain_z = diff_x(band_x, parts_x), diff_z(band_z, parts_z)
+            sxx = sxx + (both * strain_x + lame * strain_z)
+            szz = szz + (lame * strain_x + both * strain_z)
+            sxz = sxz + shear * (diff_z(band_z, parts_x) + diff_x(band_x, parts_z))
+            for component, (parts, factor) in enumerate(
+                ((parts_x, COUPLING), (parts_z, COUPLING), (halves(sxx + szz), -0.5 * COUPLING))
+            ):
+                picked = factor * (dot(parts[0], pick) + dot(parts[1], pick))
+                group = 3 * step + component
+                first = group < GROUPS
+                base, count, start = (
+                    (0, FIRST_ROWS, FIRST_AT) if first else (FIRST_ROWS, SECOND_ROWS, SECOND_AT)
+                )
+                low, high = max(start, at), min(start + count, WINDOW - at)
+                picked = picked[low - at : high - at]
+                place_at = pl.ds(base + low - start, high - low)
+                if group % GROUPS:
+                    lane = lax.broadcasted_iota(jnp.int32, picked.shape, 1) // NP
+                    picked = jnp.where(lane >= group % GROUPS, picked, rows[place_at, :])
+                rows[place_at, :] = picked
+        place([vx, vz, sxx, szz, sxz], held, sent)
+
+
+def far_kernel(
+    ids, fields, media, ahead, behind, other, rows, held_in, sent_in, held, sent, window
+):
+    section = lax.axis_index("sec")
+
+    @pl.when(section == 0)
+    def _():
+        held[...] = held_in[...]
+        sent[...] = sent_in[...]
+
+    @pl.when(section > 0)
+    def _():
+        assemble(window, fields, media, ahead, behind, other)
+        band_x = banded((WINDOW, WINDOW), -1)
+        band_z = banded((DEPTH, DEPTH), 1)
+        depth = lax.broadcasted_iota(jnp.int32, (DEPTH, CELLS), 0)
+        land = jnp.where(depth == ids[1:2, :], 1.0, 0.0).astype(jnp.bfloat16)
+        vx, vz, pressure, one, two, light, kappa, loss = [window[index] for index in range(8)]
+        light = light * (TIME_STEP / SCALE)
+        kappa = kappa * (1.0 / SCALE)
+        loss_one = loss * ((1.0 - RELAXATION[0]) * MEMORY_WEIGHT[0])
+        loss_two = loss * ((1.0 - RELAXATION[1]) * MEMORY_WEIGHT[1])
+        at = 0
+        for step in range(STEPS):
+            cut = TRIM[step] - at
+            at = TRIM[step]
+            vx, vz, pressure, one, two, light, kappa, loss_one, loss_two = trimmed(
+                [vx, vz, pressure, one, two, light, kappa, loss_one, loss_two], cut
+            )
+            parts = halves(pressure)
+            vx = vx - light * diff_x(band_x, parts)
+            vz = vz - light * diff_z(band_z, parts)
+            load = kappa * (diff_x(band_x, halves(vx)) + diff_z(band_z, halves(vz)))
+            one = RELAXATION[0] * one + loss_one * load
+            two = RELAXATION[1] * two + loss_two * load
+            pressure = pressure - TIME_STEP * (load - one - two)
+            injected = [vx, vz, pressure]
+            for component in range(3):
+                group = 3 * step + component
+                first = group < GROUPS
+                base, count, start = (
+                    (0, FIRST_ROWS, FIRST_AT) if first else (FIRST_ROWS, SECOND_ROWS, SECOND_AT)
+                )
+                low, high = max(start, at), min(start + count, WINDOW - at)
+                taken = rows[pl.ds(base + low - start, high - low), :]
+                lane = lax.broadcasted_iota(jnp.int32, taken.shape, 1) // NP
+                taken = halves(jnp.where(lane == group % GROUPS, taken, 0.0))
+                added = sum(
+                    lax.dot_general(
+                        part, land, (((1,), (1,)), ((), ())), preferred_element_type=jnp.float32
+                    )
+                    for part in taken
+                )
+                low, high = low - at, high - at
+                array = injected[component]
+                pieces = [array[:low], array[low:high] + added, array[high:]]
+                pieces = [piece for piece in pieces if piece.shape[0]]
+                injected[component] = jnp.concatenate(pieces, axis=0)
+            vx, vz, pressure = injected
+        place([vx, vz, pressure, one, two], held, sent)
+
+
+def call(kernel, outs, operands, flops):
+    vmem = pl.BlockSpec(memory_space=pltpu.VMEM)
+    return pl.pallas_call(
+        kernel,
+        out_shape=[jax.ShapeDtypeStruct(shape, jnp.float32) for shape in outs],
+        in_specs=[vmem] * len(operands),
+        out_specs=[vmem] * len(outs),
+        scratch_shapes=[pltpu.VMEM((8, WINDOW, DEPTH), jnp.float32)],
+        compiler_params=pltpu.CompilerParams(vmem_limit_bytes=48 * 1024 * 1024),
+        cost_estimate=pl.CostEstimate(
+            flops=flops, bytes_accessed=2 * 1024 * 1024, transcendentals=0
+        ),
+    )(*operands)
+
+
+def local_window(columns, fields, media, plane_rows, box_offset):
+    fields, media = fields[0], media[0]
+    core = lax.axis_index("gz")
+    is_first = core == 0
+    both = jnp.concatenate([fields, media], axis=0)
+    top, bottom = both[:, :HALO], both[:, CELLS - HALO :]
+    straight, crossed = [], []
+    for column in range(columns):
+        if column + 1 < columns:
+            straight.append((2 * column, 2 * column + 2))
+            crossed.append((2 * column + 1, 2 * column + 2))
+        if column:
+            straight.append((2 * column + 1, 2 * column - 1))
+            crossed.append((2 * column, 2 * column - 1))
+    ahead = lax.ppermute(jnp.where(is_first, bottom, top), ("gx", "gz"), straight)
+    behind = lax.ppermute(jnp.where(is_first, top, bottom), ("gx", "gz"), crossed)
+    other = lax.ppermute(
+        jnp.where(is_first, both[:, CELLS - PART :], both[:, :PART]), "gz", [(0, 1), (1, 0)]
+    )
+    section = lax.axis_index("sec")
+    offset = lax.dynamic_slice_in_dim(box_offset, jnp.maximum(section - 1, 0), 1)
+    ids = jnp.tile(jnp.stack([plane_rows, offset + plane_rows // 2]), (1, GROUPS))
+    held_shape, sent_shape = (5, CELLS, CELLS), (5, HALF, CELLS)
+    held, sent, rows = call(
+        source_kernel,
+        [held_shape, sent_shape, (ROWS, CELLS)],
+        [ids, fields, media, ahead, behind, other],
+        4_000_000_000,
+    )
+    arrived = [lax.ppermute(rows, "sec", [(0, target)]) for target in (1, 2, 3)]
+    rows = arrived[0] + arrived[1] + arrived[2]
+    held, sent = call(
+        far_kernel,
+        [held_shape, sent_shape],
+        [ids, fields, media, ahead, behind, other, rows, held, sent],
+        4_000_000_000,
+    )
+    swapped = lax.ppermute(sent, "gz", [(0, 1), (1, 0)])
+    return lax.dynamic_update_slice_in_dim(held, swapped, HALF * (1 - core), axis=1)[None]
+
+
 def solution(mesh):
     in_specs = (P("sec", None, "gx", "gz"), P("sec", None, "gx", "gz"), P(), P())
     out_specs = P("sec", None, "gx", "gz")
+    if mesh.shape["gz"] == 2:
+        local = functools.partial(local_window, mesh.shape["gx"])
+    else:
+        local = local_stepwise
     return jax.shard_map(local, mesh=mesh, in_specs=in_specs, out_specs=out_specs, check_vma=False)

time: 232 us -> 28.1 us (0.12)
  the two profiles are of different devices: /device:TPU:0 before, /device:TPU:19 now
where the time goes in v1:
time: 28.1 us; the launch traced here: 27.9 us
  waiting for transfers between devices  10.2 us (36%)
  starting transfers between devices  9.44 us (34%)
  Pallas kernels  3.54 us (13%)
  local copies, waits for them, and re-layouts  2.65 us (9%)
  other arithmetic  1.94 us (7%)
    ppermute x3, waiting for transfers between devices, local_window(): arrived = [lax.ppermute(rows, 'sec', [(0, target)]) for target in (1, 2, 3)]  7.73 us
    pallas_call x2, Pallas kernels, call(): pl.pallas_call(kernel, out_shape=[jax.ShapeDtypeStruct(shape, jnp.float32...  3.54 us
    ppermute x1, starting transfers between devices, local_window(): lax.ppermute(jnp.where(is_first, top, bottom), ('gx', 'gz'), crossed)  3.12 us
    ppermute x3, starting transfers between devices, local_window(): arrived = [lax.ppermute(rows, 'sec', [(0, target)]) for target in (1, 2, 3)]  2.62 us
    ppermute x1, starting transfers between devices, local_window(): lax.ppermute(jnp.where(is_first, bottom, top), ('gx', 'gz'), straight)  2.08 us
    ppermute x1, waiting for transfers between devices, local_window(): lax.ppermute(jnp.where(is_first, bottom, top), ('gx', 'gz'), straight)  1.41 us
    unnamed x8, local copies, waits for them, and re-layouts  1.31 us
    select_n x1, other arithmetic, local_window(): jnp.where(is_first, both[:, CELLS - PART:], both[:, :PART])  1.24 us
  transfers between devices with their start and end apart: 7, of which 3 were waited for; matrix products, arithmetic and copies ran while one was open for 5% of the time, Pallas kernels for 0%

profile of v1, /device:TPU:19, one launch (start us, length us, event | category | flops | bytes accessed | tf_op | source)
XLA Modules:
  0.0 27.9 jit_solution(13850499228509020540)
XLA Ops:
  0.0 0.0 copy-start
  0.0 0.0 copy-start.1
  0.0 1.2 %fusion.1 = f32[8,104,128]{2,1,0:T(8,128)S(1)} fusion(f32[5,128,128]{2,1,0:T(8,128)} %bitcast.9, f32[3,128,128]{2,1,0:T(8,128)} %bitcast.13, pred[]{:T(512)S(6)} %eq.3), kind=kLoop, calls=%fused_computation.7 | loop fusion | flops 319488 | bytes 950273 | tf_op jit(solution)/shard_map/jit(_where)/select_n | solution.py:398
  1.2 0.7 %collective-permute-start.2 = (f32[8,104,128]{2,1,0:T(8,128)S(1)}, f32[8,104,128]{2,1,0:T(8,128)S(1)}, u32[]{:S(2)}, u32[]{:S(2)}) collective-permute-start(f32[8,104,128]{2,1,0:T(8,128)S(1)} %fusion.1), channel_id=1, source_target_pairs={{0,1},{1,0},{2,3},{3,2},{4,5},{5,4},{6,7},{7,6},{8,9},{9,8},{10,11... | collective-permute-start | bytes 1277960 | tf_op jit(solution)/shard_map/ppermute | solution.py:397
  2.0 0.0 copy-done
  2.0 0.0 copy-done.1
  2.0 3.1 %collective-permute-start.1 = (f32[8,40,128]{2,1,0:T(8,128)S(1)}, f32[8,40,128]{2,1,0:T(8,128)S(1)}, u32[]{:S(2)}, u32[]{:S(2)}) collective-permute-start(f32[8,40,128]{2,1,0:T(8,128)S(1)} %get-tuple-element.15), channel_id=1, source_target_pairs={{1,2},{3,4},{2,1},{5,6},{4,3},{6,5},{9,10},{11,12},{10,9},{13,14},... | collective-permute-start | bytes 491528 | tf_op jit(solution)/shard_map/ppermute | solution.py:396
  5.1 2.1 %collective-permute-start = (f32[8,40,128]{2,1,0:T(8,128)S(1)}, f32[8,40,128]{2,1,0:T(8,128)S(1)}, u32[]{:S(2)}, u32[]{:S(2)}) collective-permute-start(f32[8,40,128]{2,1,0:T(8,128)S(1)} %get-tuple-element.16), channel_id=1, source_target_pairs={{0,2},{2,4},{3,1},{4,6},{5,3},{7,5},{8,10},{10,12},{11,9},{12,14},... | collective-permute-start | bytes 491528 | tf_op jit(solution)/shard_map/ppermute | solution.py:395
  7.2 0.0 copy-start.3
  7.3 0.6 %copy-done.3 = s32[3]{0:T(128)S(1)} copy-done((s32[3]{0:T(128)S(1)}, s32[3]{0:T(128)}, u32[]{:S(2)}) %copy-start.3) | copy-done | bytes 36
  7.9 0.6 %dynamic_slice.3 = s32[1]{0:T(128)} dynamic-slice(s32[3]{0:T(128)S(1)} %copy-done.3, s32[]{:T(128)S(6)} %max.3), dynamic_slice_sizes={1} | dynamic-slice | bytes 12 | tf_op jit(solution)/shard_map/dynamic_slice | solution.py:401
  8.5 0.0 copy-start.2
  8.5 0.7 %copy-done.2 = s32[16]{0:T(128)S(1)} copy-done((s32[16]{0:T(128)S(1)}, s32[16]{0:T(128)}, u32[]{:S(2)}) %copy-start.2) | copy-done | bytes 88
  9.1 0.7 %add_bitcast_fusion = s32[1,16]{1,0:T(1,128)S(1)} fusion(s32[16]{0:T(128)S(1)} %copy-done.2, s32[]{:T(128)} %bitcast.1), kind=kLoop, calls=%fused_computation.20 | loop fusion | flops 256 | bytes 132 | tf_op jit(solution)/shard_map/stack | solution.py:402
  9.8 0.1 tile.10.ids
  9.9 0.0 collective-permute-done.1.behind
  9.9 1.4 %collective-permute-done.ahead = f32[8,40,128]{2,1,0:T(8,128)S(1)} collective-permute-done((f32[8,40,128]{2,1,0:T(8,128)S(1)}, f32[8,40,128]{2,1,0:T(8,128)S(1)}, u32[]{:S(2)}, u32[]{:S(2)}) %collective-permute-start) | collective-permute-done | bytes 163872 | tf_op jit(solution)/shard_map/ppermute | solution.py:395
  11.3 0.0 collective-permute-done.2.other
  11.3 0.7 %collective-permute-start.5 = (f32[224,128]{1,0:T(8,128)S(1)}, f32[224,128]{1,0:T(8,128)S(1)}, u32[]{:S(2)}, u32[]{:S(2)}) collective-permute-start(f32[224,128]{1,0:T(8,128)S(1)} %get-tuple-element.10), channel_id=1, source_target_pairs={{0,24},{1,25},{2,26},{3,27},{4,28},{5,29},{6,30},{7,31}} | collective-permute-start | bytes 344072 | tf_op jit(solution)/shard_map/ppermute | solution.py:410
  12.0 0.7 %collective-permute-start.4 = (f32[224,128]{1,0:T(8,128)S(1)}, f32[224,128]{1,0:T(8,128)S(1)}, u32[]{:S(2)}, u32[]{:S(2)}) collective-permute-start(f32[224,128]{1,0:T(8,128)S(1)} %get-tuple-element.10), channel_id=1, source_target_pairs={{0,16},{1,17},{2,18},{3,19},{4,20},{5,21},{6,22},{7,23}} | collective-permute-start | bytes 344072 | tf_op jit(solution)/shard_map/ppermute | solution.py:410
  12.7 1.3 %collective-permute-start.3 = (f32[224,128]{1,0:T(8,128)S(1)}, f32[224,128]{1,0:T(8,128)S(1)}, u32[]{:S(2)}, u32[]{:S(2)}) collective-permute-start(f32[224,128]{1,0:T(8,128)S(1)} %get-tuple-element.10), channel_id=1, source_target_pairs={{0,8},{1,9},{2,10},{3,11},{4,12},{5,13},{6,14},{7,15}} | collective-permute-start | bytes 344072 | tf_op jit(solution)/shard_map/ppermute | solution.py:410
  14.0 0.0 collective-permute-done.5
  14.0 0.0 collective-permute-done.4
  14.0 7.7 %collective-permute-done.3 = f32[224,128]{1,0:T(8,128)S(1)} collective-permute-done((f32[224,128]{1,0:T(8,128)S(1)}, f32[224,128]{1,0:T(8,128)S(1)}, u32[]{:S(2)}, u32[]{:S(2)}) %collective-permute-start.3) | collective-permute-done | bytes 114720 | tf_op jit(solution)/shard_map/ppermute | solution.py:410
  21.7 3.5 %shard_map.47 = (f32[5,128,128]{2,1,0:T(8,128)}, f32[5,64,128]{2,1,0:T(8,128)S(1)}) custom-call(s32[2,128]{1,0:T(2,128)S(1)} %tile.10.ids, f32[5,128,128]{2,1,0:T(8,128)S(1)} %bitcast.12, f32[3,128,128]{2,1,0:T(8,128)S(1)} %bitcast.16, f32[8,40,128]{2,1,0:T(8,128)S(1)} %collective-permute-done.ahead, f32[8,40,128]{2,1,0:T(8,128)S(1)} %collective-permute-done.1.behind, ...), custom_call_target="tpu_custom_call" | custom-call | flops 4000000000 | bytes 2097152 | tf_op jit(solution)/shard_map/pallas_call | solution.py:368
  25.3 0.9 %collective-permute-start.6 = (f32[5,64,128]{2,1,0:T(8,128)S(1)}, f32[5,64,128]{2,1,0:T(8,128)S(1)}, u32[]{:S(2)}, u32[]{:S(2)}) collective-permute-start(f32[5,64,128]{2,1,0:T(8,128)S(1)} %get-tuple-element.14), channel_id=1, source_target_pairs={{0,1},{1,0},{2,3},{3,2},{4,5},{5,4},{6,7},{7,6},{8,9},{9,8},{10,11... | collective-permute-start | bytes 491528 | tf_op jit(solution)/shard_map/ppermute | solution.py:418
  26.2 1.0 %collective-permute-done.6 = f32[5,64,128]{2,1,0:T(8,128)S(1)} collective-permute-done((f32[5,64,128]{2,1,0:T(8,128)S(1)}, f32[5,64,128]{2,1,0:T(8,128)S(1)}, u32[]{:S(2)}, u32[]{:S(2)}) %collective-permute-start.6) | collective-permute-done | bytes 163872 | tf_op jit(solution)/shard_map/ppermute | solution.py:418
  27.2 0.7 %bitcast_dynamic-update-slice_fusion = f32[1,5,128,128]{3,2,1,0:T(8,128)} fusion(f32[1,5,128,128]{3,2,1,0:T(8,128)} %bitcast.18, s32[]{:T(128)S(6)} %select_n.35, f32[5,64,128]{2,1,0:T(8,128)S(1)} %collective-permute-done.6), kind=kLoop, calls=%fused_computation.11 | loop fusion | bytes 327684 | tf_op jit(solution)/shard_map/dynamic_update_slice | solution.py:419
  (5 shorter events, 0.1 us)
Async XLA Ops:
  0.0 2.0 %copy-start = (f32[1,5,128,128]{3,2,1,0:T(8,128)S(1)}, f32[1,5,128,128]{3,2,1,0:T(8,128)}, u32[]{:S(2)}) copy-start(f32[1,5,128,128]{3,2,1,0:T(8,128)} %param.4) | copy-start | bytes 983044
  0.0 2.0 %copy-start.1 = (f32[1,3,128,128]{3,2,1,0:T(8,128)S(1)}, f32[1,3,128,128]{3,2,1,0:T(8,128)}, u32[]{:S(2)}) copy-start(f32[1,3,128,128]{3,2,1,0:T(8,128)} %param.5) | copy-start | bytes 589828
  1.2 10.1 %collective-permute-start.2 = (f32[8,104,128]{2,1,0:T(8,128)S(1)}, f32[8,104,128]{2,1,0:T(8,128)S(1)}, u32[]{:S(2)}, u32[]{:S(2)}) collective-permute-start(f32[8,104,128]{2,1,0:T(8,128)S(1)} %fusion.1), channel_id=1, source_target_pairs={{0,1},{1,0},{2,3},{3,2},{4,5},{5,4},{6,7},{7,6},{8,9},{9,8},{10,11... | collective-permute-start | bytes 1277960 | tf_op jit(solution)/shard_map/ppermute | solution.py:397
  2.0 7.9 %collective-permute-start.1 = (f32[8,40,128]{2,1,0:T(8,128)S(1)}, f32[8,40,128]{2,1,0:T(8,128)S(1)}, u32[]{:S(2)}, u32[]{:S(2)}) collective-permute-start(f32[8,40,128]{2,1,0:T(8,128)S(1)} %get-tuple-element.15), channel_id=1, source_target_pairs={{1,2},{3,4},{2,1},{5,6},{4,3},{6,5},{9,10},{11,12},{10,9},{13,14},... | collective-permute-start | bytes 491528 | tf_op jit(solution)/shard_map/ppermute | solution.py:396
  5.1 6.2 %collective-permute-start = (f32[8,40,128]{2,1,0:T(8,128)S(1)}, f32[8,40,128]{2,1,0:T(8,128)S(1)}, u32[]{:S(2)}, u32[]{:S(2)}) collective-permute-start(f32[8,40,128]{2,1,0:T(8,128)S(1)} %get-tuple-element.16), channel_id=1, source_target_pairs={{0,2},{2,4},{3,1},{4,6},{5,3},{7,5},{8,10},{10,12},{11,9},{12,14},... | collective-permute-start | bytes 491528 | tf_op jit(solution)/shard_map/ppermute | solution.py:395
  7.2 0.7 %copy-start.3 = (s32[3]{0:T(128)S(1)}, s32[3]{0:T(128)}, u32[]{:S(2)}) copy-start(s32[3]{0:T(128)} %param.7) | copy-start | bytes 40
  8.5 0.7 %copy-start.2 = (s32[16]{0:T(128)S(1)}, s32[16]{0:T(128)}, u32[]{:S(2)}) copy-start(s32[16]{0:T(128)} %param.6) | copy-start | bytes 196
  11.3 2.6 %collective-permute-start.5 = (f32[224,128]{1,0:T(8,128)S(1)}, f32[224,128]{1,0:T(8,128)S(1)}, u32[]{:S(2)}, u32[]{:S(2)}) collective-permute-start(f32[224,128]{1,0:T(8,128)S(1)} %get-tuple-element.10), channel_id=1, source_target_pairs={{0,24},{1,25},{2,26},{3,27},{4,28},{5,29},{6,30},{7,31}} | collective-permute-start | bytes 344072 | tf_op jit(solution)/shard_map/ppermute | solution.py:410
  12.0 2.0 %collective-permute-start.4 = (f32[224,128]{1,0:T(8,128)S(1)}, f32[224,128]{1,0:T(8,128)S(1)}, u32[]{:S(2)}, u32[]{:S(2)}) collective-permute-start(f32[224,128]{1,0:T(8,128)S(1)} %get-tuple-element.10), channel_id=1, source_target_pairs={{0,16},{1,17},{2,18},{3,19},{4,20},{5,21},{6,22},{7,23}} | collective-permute-start | bytes 344072 | tf_op jit(solution)/shard_map/ppermute | solution.py:410
  12.7 9.0 %collective-permute-start.3 = (f32[224,128]{1,0:T(8,128)S(1)}, f32[224,128]{1,0:T(8,128)S(1)}, u32[]{:S(2)}, u32[]{:S(2)}) collective-permute-start(f32[224,128]{1,0:T(8,128)S(1)} %get-tuple-element.10), channel_id=1, source_target_pairs={{0,8},{1,9},{2,10},{3,11},{4,12},{5,13},{6,14},{7,15}} | collective-permute-start | bytes 344072 | tf_op jit(solution)/shard_map/ppermute | solution.py:410
  25.3 1.9 %collective-permute-start.6 = (f32[5,64,128]{2,1,0:T(8,128)S(1)}, f32[5,64,128]{2,1,0:T(8,128)S(1)}, u32[]{:S(2)}, u32[]{:S(2)}) collective-permute-start(f32[5,64,128]{2,1,0:T(8,128)S(1)} %get-tuple-element.14), channel_id=1, source_target_pairs={{0,1},{1,0},{2,3},{3,2},{4,5},{5,4},{6,7},{7,6},{8,9},{9,8},{10,11... | collective-permute-start | bytes 491528 | tf_op jit(solution)/shard_map/ppermute | solution.py:418
